TPU v7x, 256 devices: a whole 4x4x8 slice. The times are simulated.
256 devices in a mesh: gx: 16 (over y, x_lo, core), gy: 16 (over z, x_hi).
Axes of the slice: x: 4 (x_hi: 2, x_lo: 2; x = x_hi * 2 + x_lo), y: 4, z: 8, core: 2. Of those that a mesh axis runs over, the one named last changes fastest.
Arguments:
- eigen_block: float32 [16, 128, 256, 128], P(None, 'gx', 'gy'), may hold values from -25 to 25, as said below
- search_dirs: float32 [16, 128, 256, 128], P(None, 'gx', 'gy'), may hold values from -3 to 3
Outputs:
- new_block: float32 [16, 128, 256, 128], P(None, 'gx', 'gy')
- new_search: float32 [16, 128, 256, 128], P(None, 'gx', 'gy')
Inputs may be any that keep to these rules, and one draw needn't show every extreme that they name: `eigen_block`: real numbers whose typical size changes along the first grid dimension.
All inputs are finite; a program needn't handle non-finite values.
Results may differ from a plain program's by a relative error of at most 0.0003.
Values sent between devices are 32-bit elements; how exact they have to be, the bound alone decides.
A program may use at most 64 MiB of HBM per device.

v0:
```python
import functools

import jax
import jax.numpy as jnp
from jax import lax
from jax.experimental import pallas as pl
from jax.experimental.pallas import tpu as pltpu
from jax.sharding import PartitionSpec as P

MESH = pl.DeviceIdType.MESH
HP = lax.Precision.HIGHEST
F32 = jnp.float32
BF16 = jnp.bfloat16

K = 16
NX, NY, NZ = 8, 16, 128
H = 4
CX, CY = NX // 2, NY // 2
HC = 3
HD = 2
SHIFT = 13.0

DIRS = [(-1, 0), (1, 0), (0, -1), (0, 1), (-1, -1), (-1, 1), (1, -1), (1, 1)]


def masks_of(bits):
    out = [(0, 0)]
    for bx, by in bits:
        out = out + [(x | bx, y | by) for x, y in out]
    return out[1:]


CORE = masks_of([(1, 0)])
PLANE = masks_of([(2, 0), (0, 1), (4, 0), (8, 0)])
DEPTH = masks_of([(0, 2), (0, 4), (0, 8)])


def span(step, layers, size, offset):
    if step == 0:
        return (offset, offset, size)
    first, last = layers
    count = last - first + 1
    if step < 0:
        return (offset + first - 1, offset + size + first - 1, count)
    return (offset + size - last, offset - last, count)


def transfers():
    groups = {}
    groups["x1"] = [("x", d, (1, 1), (1, 1)) for d in range(4)]
    deep = [("x", d, (2, 4), (2, 4)) for d in range(4)]
    for d in range(4, 8):
        deep += [("x", d, (1, 1), (1, 3)), ("x", d, (2, 2), (1, 2)), ("x", d, (3, 3), (1, 1))]
    groups["x4"] = deep
    groups["p1"] = [("p", d, (1, 1), (1, 1)) for d in range(4)]
    rough = [("cr", d, (1, 3), (1, 3)) for d in range(4)]
    for d in range(4, 8):
        rough += [("cr", d, (1, 1), (1, 2)), ("cr", d, (2, 2), (1, 1))]
    groups["cr"] = rough
    groups["e"] = [("e", d, (2, 3), (2, 3)) for d in range(4)] + [("e", d, (1, 2), (1, 2)) for d in range(4, 8)]
    groups["c"] = [("c", d, (1, 2), (1, 2)) for d in range(4)] + [("c", d, (1, 1), (1, 1)) for d in range(4, 8)]
    return groups


GROUPS = transfers()
FIRST = {}
COUNT = 0
for _name in GROUPS:
    FIRST[_name] = COUNT
    COUNT += len(GROUPS[_name])

GEOMETRY = {"x": (NX, NY, H), "p": (NX, NY, 1), "e": (NX, NY, H), "cr": (CX, CY, HC), "c": (CX, CY, HD)}


def tree(parts):
    while len(parts) > 1:
        parts = [parts[i] + parts[i + 1] for i in range(0, len(parts), 2)]
    return parts[0]


def chunks(start, stop, width=4):
    return [(j, min(width, stop - j)) for j in range(start, stop, width)]


def kernel(
    x_hbm, p_hbm, block_hbm, search_hbm,
    x_nat, p_nat, x_ext, p_ext, r_ext, ea, eb, ec, crp, ca, cb, cd, split, out_block, out_search,
    th_mine, th_core, th_plane, th_depth, ar_mine, ar_core, ar_plane, ar_depth, ar_full,
    send_sem, recv_sem, red_send, red_recv, local_sem,
):
    gx, gy = lax.axis_index("gx"), lax.axis_index("gy")
    nx, ny = lax.axis_size("gx"), lax.axis_size("gy")
    core = lax.rem(gx, 2)
    load_x = pltpu.make_async_copy(x_hbm, x_nat, local_sem.at[0])
    load_p = pltpu.make_async_copy(p_hbm, p_nat, local_sem.at[1])
    load_x.start()
    load_p.start()

    buffers = {"x": x_ext, "p": p_ext, "e": ec, "cr": crp, "c": cd}
    lane = lax.broadcasted_iota(jnp.int32, (1, 1, NZ), 2)
    first_z, last_z, even = lane == 0, lane == NZ - 1, lane % 2 == 0

    def exists(d, sign):
        dx, dy = DIRS[d]
        tests = []
        if dx:
            tests.append(gx > 0 if dx * sign < 0 else gx < nx - 1)
        if dy:
            tests.append(gy > 0 if dy * sign < 0 else gy < ny - 1)
        return functools.reduce(jnp.logical_and, tests)

    def copy_of(name, index):
        key, d, rows, cols = GROUPS[name][index]
        dx, dy = DIRS[d]
        sx, sy, offset = GEOMETRY[key]
        rs, rd, rn = span(dx, rows, sx, offset)
        cs, cd_, cn = span(dy, cols, sy, offset)
        buf = buffers[key]
        sem = FIRST[name] + index
        return d, pltpu.make_async_remote_copy(
            src_ref=buf.at[pl.ds(rs, rn), pl.ds(cs, cn)],
            dst_ref=buf.at[pl.ds(rd, rn), pl.ds(cd_, cn)],
            send_sem=send_sem.at[sem],
            recv_sem=recv_sem.at[sem],
            device_id=(gx + dx, gy + dy),
            device_id_type=MESH,
        )

    def send(name):
        for index in range(len(GROUPS[name])):
            d, copy = copy_of(name, index)
            pl.when(exists(d, 1))(copy.start)

    def receive(name):
        for index in range(len(GROUPS[name])):
            d, copy = copy_of(name, index)
            pl.when(exists(d, -1))(copy.wait_recv)

    def sent(name):
        for index in range(len(GROUPS[name])):
            d, copy = copy_of(name, index)
            pl.when(exists(d, 1))(copy.wait_send)

    def exchange(masks, base, source, slots):
        copies = [
            pltpu.make_async_remote_copy(
                src_ref=source,
                dst_ref=slots.at[i],
                send_sem=red_send.at[base + i],
                recv_sem=red_recv.at[base + i],
                device_id=(gx ^ mx, gy ^ my),
                device_id_type=MESH,
            )
            for i, (mx, my) in enumerate(masks)
        ]
        for copy in copies:
            copy.start()
        for copy in copies:
            copy.wait_send()
            copy.wait_recv()

    def clear(ref, rows):
        def row(i, carry):
            ref[i] = jnp.zeros(ref.shape[1:], ref.dtype)
            return carry
        lax.fori_loop(0, rows, row, 0)

    clear(x_ext, NX + 2 * H)
    clear(p_ext, NX + 2)
    clear(ec, NX + 2 * H)
    clear(crp, CX + 2 * HC)
    clear(cd, CX + 2 * HD)

    barrier = pltpu.get_barrier_semaphore()
    expected = 0
    for d in range(8):
        dx, dy = DIRS[d]
        there = exists(d, 1)

        @pl.when(there)
        def _():
            pl.semaphore_signal(barrier, inc=1, device_id=(gx + dx, gy + dy), device_id_type=MESH)

        expected = expected + jnp.where(there, 1, 0)
    partners = CORE + PLANE + DEPTH
    for mx, my in partners:
        pl.semaphore_signal(barrier, inc=1, device_id=(gx ^ mx, gy ^ my), device_id_type=MESH)

    clear(r_ext, NX + 2 * H)
    clear(ea, NX + 2 * H)
    clear(eb, NX + 2 * H)
    clear(ca, CX + 2 * HC)
    clear(cb, CX + 2 * HC)

    def put(cell, row, value):
        high = value.astype(BF16)
        split[cell, pl.ds(row, K)] = high
        split[cell, pl.ds(row + 128, K)] = (value - high.astype(F32)).astype(BF16)

    load_x.wait()

    def bring_x(i, carry):
        for j in range(NY):
            value = x_nat[pl.ds(i * NY + j, K, stride=NX * NY), :]
            x_ext[i + H, j + H] = value
        return carry

    lax.fori_loop(0, NX, bring_x, 0)
    pl.semaphore_wait(barrier, expected + len(partners))
    send("x1")
    send("x4")
    load_p.wait()

    def bring_p(i, carry):
        for j in range(NY):
            p_ext[i + 1, j + 1] = p_nat[pl.ds(i * NY + j, K, stride=NX * NY), :]
        return carry

    lax.fori_loop(0, NX, bring_p, 0)
    send("p1")

    def keep(i, carry):
        for j in range(NY):
            cell = i * NY + j
            put(cell, 0, x_ext[i + H, j + H])
            put(cell, 16, p_ext[i + 1, j + 1])
            split[cell, pl.ds(96, 32)] = jnp.zeros((32, NZ), BF16)
            split[cell, pl.ds(224, 32)] = jnp.zeros((32, NZ), BF16)
        return carry

    lax.fori_loop(0, NX, keep, 0)

    def beside_z(center, step):
        zero = jnp.zeros_like(center)
        if step == 1:
            down = jnp.where(first_z, zero, pltpu.roll(center, 1, 2))
            up = jnp.where(last_z, zero, pltpu.roll(center, NZ - 1, 2))
        else:
            down = jnp.where(lane < 2, zero, pltpu.roll(center, 2, 2))
            up = jnp.where(lane >= NZ - 2, zero, pltpu.roll(center, NZ - 2, 2))
        return down + up

    def around(ref, i, j, n, step=1):
        center = ref[i, pl.ds(j, n)]
        beside = ref[i - 1, pl.ds(j, n)] + ref[i + 1, pl.ds(j, n)]
        beside = beside + (ref[i, pl.ds(j - 1, n)] + ref[i, pl.ds(j + 1, n)])
        return center, beside + beside_z(center, step)

    left = jnp.where(gy > 0, 1.0, 0.0).astype(F32)
    right = jnp.where(gy < ny - 1, 1.0, 0.0).astype(F32)

    def sweep(depth, sizes, offset, body, width=4):
        sx, sy = sizes
        low = jnp.where(gx > 0, offset - depth, offset)
        high = jnp.where(gx < nx - 1, offset + sx + depth, offset + sx)

        def row(i, carry):
            if depth:
                body(i, offset - depth, depth, left)
            for j, n in chunks(offset, offset + sy, width):
                body(i, j, n, None)
            if depth:
                body(i, offset + sy, depth, right)
            return carry

        lax.fori_loop(low, high, row, 0)

    def scaled(value, scale):
        return value if scale is None else value * scale

    receive("x1")

    def image_x(i, carry):
        numer, denom = carry
        for j, n in chunks(H, H + NY):
            center, beside = around(x_ext, i + H, j, n)
            image = 6.0 * center - beside
            for q in range(n):
                put(i * NY + j - H + q, 48, image[q])
            numer = numer + jnp.sum(center * image, axis=0)
            denom = denom + jnp.sum(center * center, axis=0)
        return numer, denom

    zero = jnp.zeros((K, NZ), F32)
    numer, denom = lax.fori_loop(0, NX, image_x, (zero, zero))
    numer = jnp.sum(numer, axis=1, keepdims=True)
    denom = jnp.sum(denom, axis=1, keepdims=True)
    lane2 = lax.broadcasted_iota(jnp.int32, (K, NZ), 1)
    th_mine[0] = jnp.where(lane2 < 64, numer, denom)
    exchange(CORE, 0, th_mine.at[0], th_core)
    th_mine[1] = th_mine[0] + th_core[0]
    exchange(PLANE, 1, th_mine.at[1], th_plane)
    th_mine[2] = tree([th_mine[1]] + [th_plane[i] for i in range(15)])
    exchange(DEPTH, 16, th_mine.at[2], th_depth)
    total = tree([th_mine[2]] + [th_depth[i] for i in range(7)])
    theta = (total / pltpu.roll(total, 64, 1))[:, 0:1]
    theta = jnp.broadcast_to(theta, (K, NZ))

    receive("p1")

    def image_p(i, carry):
        for j, n in chunks(1, 1 + NY):
            center, beside = around(p_ext, i + 1, j, n)
            image = 6.0 * center - beside
            for q in range(n):
                put(i * NY + j - 1 + q, 64, image[q])
        return carry

    lax.fori_loop(0, NX, image_p, 0)
    receive("x4")

    def residual(i, j, n, scale):
        center, beside = around(x_ext, i, j, n)
        r_ext[i, pl.ds(j, n)] = scaled((6.0 - theta) * center - beside, scale)

    sweep(3, (NX, NY), H, residual)

    def first_sweep(i, j, n, scale):
        center, beside = around(r_ext, i, j, n)
        eb[i, pl.ds(j, n)] = scaled((12.0 * center + beside) * (1.0 / 81.0), scale)

    sweep(2, (NX, NY), H, first_sweep)

    def smoothed(source, i, j, n):
        center, beside = around(source, i, j, n)
        return center * (1.0 / 3.0) + (r_ext[i, pl.ds(j, n)] + beside) * (1.0 / 9.0)

    def second_sweep(i, j, n, scale):
        ec[i, pl.ds(j, n)] = scaled(smoothed(eb, i, j, n), scale)

    def second_row(i):
        for j, n in chunks(H, H + NY):
            second_sweep(i, j, n, None)

    sweep_rows = (H, H + NX)

    def second_inner(i, carry):
        second_sweep(i, H - 1, 1, left)
        for j, n in chunks(H, H + NY):
            second_sweep(i, j, n, None)
        second_sweep(i, H + NY, 1, right)
        return carry

    lax.fori_loop(sweep_rows[0], sweep_rows[1], second_inner, 0)
    pl.when(gx > 0)(lambda: second_row(H - 1))
    pl.when(gx < nx - 1)(lambda: second_row(H + NX))

    def restrict(ci, carry):
        for j, n in chunks(H, H + NY):
            total = None
            for half in range(2):
                i = 2 * ci + half + H
                center, beside = around(ec, i, j, n)
                rest = r_ext[i, pl.ds(j, n)] - 6.0 * center + beside
                total = rest if total is None else total + rest
            for q in range(0, n, 2):
                cube = total[q] + total[q + 1]
                low, high = cube[0:8], cube[8:16]
                low = low + pltpu.roll(low, NZ - 1, 1)
                high = high + pltpu.roll(high, 1, 1)
                crp[ci + HC, (j - H + q) // 2 + HC] = jnp.where(even[0], low, high)
        return carry

    lax.fori_loop(0, CX, restrict, 0)
    send("cr")
    send("e")

    receive("cr")

    def coarse_first(i, j, n, scale):
        center, beside = around(crp, i, j, n, 2)
        ca[i, pl.ds(j, n)] = scaled(center * (1.0 / 27.0) + beside * (1.0 / 324.0), scale)

    def coarse_next(source, target, shift):
        def body(i, j, n, scale):
            center, beside = around(source, i, j, n, 2)
            value = center * (1.0 / 3.0) + crp[i, pl.ds(j, n)] * (1.0 / 36.0) + beside * (1.0 / 9.0)
            target[i - shift, pl.ds(j - shift, n)] = scaled(value, scale)
        return body

    sweep(2, (CX, CY), HC, coarse_first)
    sweep(1, (CX, CY), HC, coarse_next(ca, cb, 0))
    sweep(0, (CX, CY), HC, coarse_next(cb, cd, HC - HD))
    send("c")
    receive("e")
    receive("c")

    def correct(ci, carry):
        for cj in range(CY + 2 * HD):
            packed = cd[ci, cj]
            low = jnp.where(even[0], packed, pltpu.roll(packed, 1, 1))
            high = jnp.where(even[0], pltpu.roll(packed, NZ - 1, 1), packed)
            both = jnp.concatenate([low, high], axis=0)
            for half in range(2):
                i = 2 * ci + half
                ea[i, pl.ds(2 * cj, 2)] = ec[i, pl.ds(2 * cj, 2)] + both[None]
        return carry

    lax.fori_loop(0, CX + 2 * HD, correct, 0)

    def third_sweep(i, j, n, scale):
        eb[i, pl.ds(j, n)] = scaled(smoothed(ea, i, j, n), scale)

    def fourth_sweep(i, j, n, scale):
        ea[i, pl.ds(j, n)] = scaled(smoothed(eb, i, j, n), scale)

    sweep(2, (NX, NY), H, third_sweep)
    sweep(1, (NX, NY), H, fourth_sweep)

    def image_w(i, carry):
        for j, n in chunks(H, H + NY):
            center, beside = around(ea, i + H, j, n)
            image = 6.0 * center - beside
            for q in range(n):
                put(i * NY + j - H + q, 32, center[q])
                put(i * NY + j - H + q, 80, image[q])
        return carry

    lax.fori_loop(0, NX, image_w, 0)

    def products(i, acc):
        for j in range(0, NY, 2):
            cell = i * NY + j
            rhs = jnp.concatenate([split[cell], split[cell + 1]], axis=1)
            lhs = jnp.concatenate([rhs[0:48], rhs[128:176]], axis=0)
            acc = acc + lax.dot_general(lhs, rhs, (((1,), (1,)), ((), ())), preferred_element_type=F32)
        return acc

    acc = lax.fori_loop(0, NX, products, jnp.zeros((96, 256), F32))
    part = (acc[0:48, 0:128] + acc[0:48, 128:256]) + (acc[48:96, 0:128] + acc[48:96, 128:256])
    ar_mine[0] = part[0:24]
    ar_mine[1] = part[24:48]
    exchange(CORE, 23, ar_mine.at[1 - core], ar_core)
    ar_mine[2] = ar_mine[core] + ar_core[0]
    exchange(PLANE, 24, ar_mine.at[2], ar_plane)
    ar_mine[3] = tree([ar_mine[2]] + [ar_plane[i] for i in range(15)])
    exchange(DEPTH, 39, ar_mine.at[3], ar_depth)
    ar_full[core] = tree([ar_mine[3]] + [ar_depth[i] for i in range(7)])
    swap = pltpu.make_async_remote_copy(
        src_ref=ar_full.at[core],
        dst_ref=ar_full.at[core],
        send_sem=red_send.at[46],
        recv_sem=red_recv.at[46],
        device_id=(gx ^ 1, gy),
        device_id_type=MESH,
    )
    swap.start()
    swap.wait_send()
    swap.wait_recv()

    both = jnp.concatenate([ar_full[0], ar_full[1]], axis=0)

    def inverse_factor(matrix, size):
        rows = lax.broadcasted_iota(jnp.int32, (size, NZ), 0)
        lanes = lax.broadcasted_iota(jnp.int32, (size, NZ), 1)
        start = jnp.where(lanes < size, matrix, jnp.where(lanes == rows + 64, 1.0, 0.0))
        tiles = [start[8 * t : 8 * t + 8] for t in range(size // 8)]
        sub = lax.broadcasted_iota(jnp.int32, (8, NZ), 0)
        for k in range(size):
            t0, s0 = k // 8, k % 8
            pivot = tiles[t0][s0 : s0 + 1]
            pivot = pivot / pivot[:, k : k + 1]
            for t in range(t0, size // 8):
                column = jnp.broadcast_to(tiles[t][:, k : k + 1], (8, NZ))
                if t == t0:
                    column = jnp.where(sub > s0, column, 0.0)
                tiles[t] = tiles[t] - column * pivot
        done = jnp.concatenate(tiles, axis=0)
        diagonal = jnp.sum(jnp.where(lanes == rows, done, 0.0), axis=1, keepdims=True)
        return pltpu.roll(done / jnp.sqrt(diagonal), 64, 1)[:, 0:size]

    def dot(a, b):
        return jnp.dot(a, b, precision=HP, preferred_element_type=F32)

    def dot_t(a, b):
        return lax.dot_general(a, b, (((1,), (1,)), ((), ())), precision=HP, preferred_element_type=F32)

    proj = pltpu.roll(both, NZ - 48, 1)[:, 0:48]
    proj = 0.5 * (proj + proj.T)
    lower_inv = inverse_factor(both, 48)
    ritz = dot_t(dot(lower_inv, proj), lower_inv)
    ritz = 0.5 * (ritz + ritz.T)
    rows = lax.broadcasted_iota(jnp.int32, (K, 48), 0)
    cols = lax.broadcasted_iota(jnp.int32, (K, 48), 1)
    filtered_t = jnp.where(rows == cols, SHIFT, 0.0) - ritz[0:K]
    square = dot_t(filtered_t, filtered_t)
    square = jnp.concatenate([square, jnp.zeros((K, NZ - K), F32)], axis=1)
    small_inv = inverse_factor(square, K)
    ncells = float(NX * NY * NZ * nx * ny)
    coef_t = dot(dot(small_inv, filtered_t), lower_inv) * (ncells**0.5)

    coef_t = jnp.concatenate([coef_t, jnp.where(cols < K, 0.0, coef_t)], axis=0)
    coef_t = jnp.concatenate([coef_t, jnp.zeros((2 * K, NZ - 48), F32)], axis=1)
    high = coef_t.astype(BF16)
    low = (coef_t - high.astype(F32)).astype(BF16)
    weights = jnp.concatenate([high, low], axis=0)
    weights = jnp.concatenate([weights, weights], axis=1)

    def combine(i, carry):
        for j in range(0, NY, 2):
            cell = i * NY + j
            rhs = jnp.concatenate([split[cell], split[cell + 1]], axis=1)
            out = jnp.dot(weights, rhs, preferred_element_type=F32)
            out = out[0:32] + out[32:64]
            for q in range(2):
                out_block[pl.ds(cell + q, K, stride=NX * NY), :] = out[0:16, 128 * q : 128 * q + 128]
                out_search[pl.ds(cell + q, K, stride=NX * NY), :] = out[16:32, 128 * q : 128 * q + 128]
        return carry

    lax.fori_loop(0, NX, combine, 0)
    save_block = pltpu.make_async_copy(out_block, block_hbm, local_sem.at[0])
    save_search = pltpu.make_async_copy(out_search, search_hbm, local_sem.at[1])
    save_block.start()
    save_search.start()
    for name in GROUPS:
        sent(name)
    save_block.wait()
    save_search.wait()


def body(eigen_block, search_dirs):
    shape = eigen_block.shape
    flat = (shape[0] * shape[1] * shape[2], shape[3])
    vmem = pltpu.VMEM
    fine = (NX + 2 * H, NY + 2 * H, K, NZ)
    rough = (CX + 2 * HC, CY + 2 * HC, K // 2, NZ)
    scratch = [
        vmem(flat, F32),
        vmem(flat, F32),
        vmem(fine, F32),
        vmem((NX + 2, NY + 2, K, NZ), F32),
        vmem(fine, F32),
        vmem(fine, F32),
        vmem(fine, F32),
        vmem(fine, F32),
        vmem(rough, F32),
        vmem(rough, F32),
        vmem(rough, F32),
        vmem((CX + 2 * HD, CY + 2 * HD, K // 2, NZ), F32),
        vmem((NX * NY, 256, NZ), BF16),
        vmem(flat, F32),
        vmem(flat, F32),
        vmem((3, K, NZ), F32),
        vmem((1, K, NZ), F32),
        vmem((15, K, NZ), F32),
        vmem((7, K, NZ), F32),
        vmem((4, 24, NZ), F32),
        vmem((1, 24, NZ), F32),
        vmem((15, 24, NZ), F32),
        vmem((7, 24, NZ), F32),
        vmem((2, 24, NZ), F32),
        pltpu.SemaphoreType.DMA((COUNT,)),
        pltpu.SemaphoreType.DMA((COUNT,)),
        pltpu.SemaphoreType.DMA((47,)),
        pltpu.SemaphoreType.DMA((47,)),
        pltpu.SemaphoreType.DMA((2,)),
    ]
    block, search = pl.pallas_call(
        kernel,
        out_shape=(jax.ShapeDtypeStruct(flat, F32), jax.ShapeDtypeStruct(flat, F32)),
        in_specs=[pl.BlockSpec(memory_space=pl.ANY)] * 2,
        out_specs=(pl.BlockSpec(memory_space=pl.ANY), pl.BlockSpec(memory_space=pl.ANY)),
        scratch_shapes=scratch,
        compiler_params=pltpu.CompilerParams(
            collective_id=0, has_side_effects=True, vmem_limit_bytes=56 * 1024 * 1024
        ),
    )(eigen_block.reshape(flat), search_dirs.reshape(flat))
    return block.reshape(shape), search.reshape(shape)


def solution(mesh):
    spec = P(None, "gx", "gy", None)
    return jax.shard_map(body, mesh=mesh, in_specs=(spec, spec), out_specs=(spec, spec), check_vma=False)
```

profile of v0, /device:TPU:1, one launch (start us, length us, event | category | flops | bytes accessed | tf_op | source)
XLA Modules:
  0.0 118.8 jit_solution(8137678588106909085)
XLA Ops:
  0.6 114.8 %shard_map.41 = (f32[2048,128]{1,0:T(8,128)}, f32[2048,128]{1,0:T(8,128)}) custom-call(f32[2048,128]{1,0:T(8,128)} %bitcast.4, f32[2048,128]{1,0:T(8,128)} %bitcast.5), custom_call_target="tpu_custom_call" | custom-call | tf_op jit(solution)/shard_map/pallas_call | solution.py:558
  115.4 0.0 copy-start
  115.4 2.4 %copy.6 = f32[16,8,16,128]{3,2,1,0:T(8,128)} copy(f32[16,8,16,128]{3,2,1,0:T(8,128)} %bitcast.7) | data formatting | bytes 2097152
  117.8 0.0 copy-done
  117.8 1.0 copy.7
Async XLA Ops:
  115.4 2.4 %copy-start = (f32[2048,128]{1,0:T(8,128)S(1)}, f32[2048,128]{1,0:T(8,128)}, u32[]{:S(2)}) copy-start(f32[2048,128]{1,0:T(8,128)} %get-tuple-element.5) | copy-start | bytes 3145732
where the time goes:
time: 119 us
  Pallas kernels  115 us (97%)
  local copies, waits for them, and re-layouts  3.36 us (3%)
    pallas_call x1, Pallas kernels, body(): pl.pallas_call(kernel, out_shape=(jax.ShapeDtypeStruct(flat, F32), jax.Sh...  115 us
    unnamed x4, local copies, waits for them, and re-layouts  3.36 us

commit v1 on v0

--- a/solution.py
+++ b/solution.py
@@ -16,9 +16,10 @@
 NX, NY, NZ = 8, 16, 128
 H = 4
 CX, CY = NX // 2, NY // 2
-HC = 3
-HD = 2
+HC = 4
+HD = 1
 SHIFT = 13.0
+X, PD, IX, IP, W, IW = 0, 16, 32, 48, 64, 80
 
 DIRS = [(-1, 0), (1, 0), (0, -1), (0, 1), (-1, -1), (-1, 1), (1, -1), (1, 1)]
 
@@ -48,17 +49,21 @@
 def transfers():
     groups = {}
     groups["x1"] = [("x", d, (1, 1), (1, 1)) for d in range(4)]
-    deep = [("x", d, (2, 4), (2, 4)) for d in range(4)]
+    groups["x2"] = [("x", d, (2, 2), (2, 2)) for d in range(4)] + [("x", d, (1, 1), (1, 1)) for d in range(4, 8)]
+    deep = [("x", d, (3, 4), (3, 4)) for d in range(4)]
     for d in range(4, 8):
-        deep += [("x", d, (1, 1), (1, 3)), ("x", d, (2, 2), (1, 2)), ("x", d, (3, 3), (1, 1))]
+        deep += [("x", d, (1, 1), (2, 3)), ("x", d, (2, 2), (1, 2)), ("x", d, (3, 3), (1, 1))]
     groups["x4"] = deep
-    groups["p1"] = [("p", d, (1, 1), (1, 1)) for d in range(4)]
-    rough = [("cr", d, (1, 3), (1, 3)) for d in range(4)]
+    groups["p1"] = [("p", d, (1, 1), (1, 1)) for d in (1, 3)]
+    groups["w1"] = [("w", d, (1, 1), (1, 1)) for d in (1, 3)]
+    rough = [("cr", d, (1, 4), (1, 4)) for d in range(4)]
     for d in range(4, 8):
-        rough += [("cr", d, (1, 1), (1, 2)), ("cr", d, (2, 2), (1, 1))]
+        rough += [("cr", d, (1, 1), (1, 3)), ("cr", d, (2, 2), (1, 2)), ("cr", d, (3, 3), (1, 1))]
     groups["cr"] = rough
-    groups["e"] = [("e", d, (2, 3), (2, 3)) for d in range(4)] + [("e", d, (1, 2), (1, 2)) for d in range(4, 8)]
-    groups["c"] = [("c", d, (1, 2), (1, 2)) for d in range(4)] + [("c", d, (1, 1), (1, 1)) for d in range(4, 8)]
+    sums = [("s", d, (3, 3), (3, 3)) for d in range(4)]
+    for d in range(4, 8):
+        sums += [("s", d, (1, 1), (2, 2)), ("s", d, (2, 2), (1, 1))]
+    groups["s"] = sums
     return groups
 
 
@@ -69,7 +74,7 @@
     FIRST[_name] = COUNT
     COUNT += len(GROUPS[_name])
 
-GEOMETRY = {"x": (NX, NY, H), "p": (NX, NY, 1), "e": (NX, NY, H), "cr": (CX, CY, HC), "c": (CX, CY, HD)}
+GEOMETRY = {"x": (NX, NY, H), "p": (NX, NY, 1), "w": (NX, NY, 1), "s": (NX, NY, H), "cr": (CX, CY, HC)}
 
 
 def tree(parts):
@@ -84,7 +89,7 @@
 
 def kernel(
     x_hbm, p_hbm, block_hbm, search_hbm,
-    x_nat, p_nat, x_ext, p_ext, r_ext, ea, eb, ec, crp, ca, cb, cd, split, out_block, out_search,
+    x_nat, p_nat, x_ext, p_ext, w_ext, r_ext, ea, eb, ec, s_ext, crp, ca, cb, cd, split, out_block, out_search,
     th_mine, th_core, th_plane, th_depth, ar_mine, ar_core, ar_plane, ar_depth, ar_full,
     send_sem, recv_sem, red_send, red_recv, local_sem,
 ):
@@ -96,7 +101,7 @@
     load_x.start()
     load_p.start()
 
-    buffers = {"x": x_ext, "p": p_ext, "e": ec, "cr": crp, "c": cd}
+    buffers = {"x": x_ext, "p": p_ext, "s": s_ext, "cr": crp, "w": w_ext}
     lane = lax.broadcasted_iota(jnp.int32, (1, 1, NZ), 2)
     first_z, last_z, even = lane == 0, lane == NZ - 1, lane % 2 == 0
 
@@ -155,23 +160,54 @@
         ]
         for copy in copies:
             copy.start()
-        for copy in copies:
-            copy.wait_send()
-            copy.wait_recv()
-
-    def clear(ref, rows):
-        def row(i, carry):
-            ref[i] = jnp.zeros(ref.shape[1:], ref.dtype)
-            return carry
-        lax.fori_loop(0, rows, row, 0)
-
-    clear(x_ext, NX + 2 * H)
-    clear(p_ext, NX + 2)
-    clear(ec, NX + 2 * H)
-    clear(crp, CX + 2 * HC)
-    clear(cd, CX + 2 * HD)
+
+        def finish():
+            for copy in copies:
+                copy.wait_send()
+                copy.wait_recv()
+
+        return finish
 
     barrier = pltpu.get_barrier_semaphore()
+    partners = CORE + PLANE + DEPTH
+    for mx, my in partners:
+        pl.semaphore_signal(barrier, inc=1, device_id=(gx ^ mx, gy ^ my), device_id_type=MESH)
+
+    def clear(ref, offset, always=False):
+        rows, cols = ref.shape[:2]
+
+        def block(i, j, n, m):
+            ref[pl.ds(i, n), pl.ds(j, m)] = jnp.zeros((n, m) + tuple(ref.shape[2:]), ref.dtype)
+
+        def lines(first):
+            def line(i, carry):
+                block(i, 0, 1, cols)
+                return carry
+            lax.fori_loop(first, first + offset, line, 0)
+
+        def columns(first):
+            def line(i, carry):
+                block(i, first, 1, offset)
+                return carry
+            lax.fori_loop(0, rows, line, 0)
+
+        def where(test, fill, first):
+            if always:
+                fill(first)
+            else:
+                pl.when(test)(lambda: fill(first))
+
+        where(gx == 0, lines, 0)
+        where(gx == nx - 1, lines, rows - offset)
+        where(gy == 0, columns, 0)
+        where(gy == ny - 1, columns, cols - offset)
+
+    clear(x_ext, H)
+    clear(p_ext, 1, always=True)
+    clear(w_ext, 1, always=True)
+    clear(s_ext, H)
+    clear(crp, HC)
+
     expected = 0
     for d in range(8):
         dx, dy = DIRS[d]
@@ -182,15 +218,7 @@
             pl.semaphore_signal(barrier, inc=1, device_id=(gx + dx, gy + dy), device_id_type=MESH)
 
         expected = expected + jnp.where(there, 1, 0)
-    partners = CORE + PLANE + DEPTH
-    for mx, my in partners:
-        pl.semaphore_signal(barrier, inc=1, device_id=(gx ^ mx, gy ^ my), device_id_type=MESH)
-
-    clear(r_ext, NX + 2 * H)
-    clear(ea, NX + 2 * H)
-    clear(eb, NX + 2 * H)
-    clear(ca, CX + 2 * HC)
-    clear(cb, CX + 2 * HC)
+
 
     def put(cell, row, value):
         high = value.astype(BF16)
@@ -208,8 +236,15 @@
     lax.fori_loop(0, NX, bring_x, 0)
     pl.semaphore_wait(barrier, expected + len(partners))
     send("x1")
-    send("x4")
+    send("x2")
     load_p.wait()
+    clear(r_ext, H)
+    clear(ea, H)
+    clear(eb, H)
+    clear(ec, H)
+    clear(ca, HC)
+    clear(cb, HC)
+    clear(cd, HD)
 
     def bring_p(i, carry):
         for j in range(NY):
@@ -217,13 +252,12 @@
         return carry
 
     lax.fori_loop(0, NX, bring_p, 0)
-    send("p1")
 
     def keep(i, carry):
         for j in range(NY):
             cell = i * NY + j
-            put(cell, 0, x_ext[i + H, j + H])
-            put(cell, 16, p_ext[i + 1, j + 1])
+            put(cell, X, x_ext[i + H, j + H])
+            put(cell, PD, p_ext[i + 1, j + 1])
             split[cell, pl.ds(96, 32)] = jnp.zeros((32, NZ), BF16)
             split[cell, pl.ds(224, 32)] = jnp.zeros((32, NZ), BF16)
         return carry
@@ -241,9 +275,10 @@
         return down + up
 
     def around(ref, i, j, n, step=1):
-        center = ref[i, pl.ds(j, n)]
+        line = ref[i, pl.ds(j - 1, n + 2)]
+        center = line[1 : n + 1]
         beside = ref[i - 1, pl.ds(j, n)] + ref[i + 1, pl.ds(j, n)]
-        beside = beside + (ref[i, pl.ds(j - 1, n)] + ref[i, pl.ds(j + 1, n)])
+        beside = beside + (line[0:n] + line[2 : n + 2])
         return center, beside + beside_z(center, step)
 
     left = jnp.where(gy > 0, 1.0, 0.0).astype(F32)
@@ -276,7 +311,7 @@
             center, beside = around(x_ext, i + H, j, n)
             image = 6.0 * center - beside
             for q in range(n):
-                put(i * NY + j - H + q, 48, image[q])
+                put(i * NY + j - H + q, IX, image[q])
             numer = numer + jnp.sum(center * image, axis=0)
             denom = denom + jnp.sum(center * center, axis=0)
         return numer, denom
@@ -285,73 +320,88 @@
     numer, denom = lax.fori_loop(0, NX, image_x, (zero, zero))
     numer = jnp.sum(numer, axis=1, keepdims=True)
     denom = jnp.sum(denom, axis=1, keepdims=True)
+
+    def pair(cell, row, count):
+        return jnp.concatenate([split[cell, pl.ds(row, count)], split[cell + 1, pl.ds(row, count)]], axis=1)
+
+    def product(lhs, rhs, acc):
+        return acc + lax.dot_general(lhs, rhs, (((1,), (1,)), ((), ())), preferred_element_type=F32)
+
+    def early_products(i, acc):
+        for j in range(0, NY, 2):
+            cell = i * NY + j
+            high, low = pair(cell, X, 48), pair(cell, X + 128, 48)
+            rhs = jnp.concatenate([high, low], axis=0)
+            lhs = jnp.concatenate([high[0:32], low[0:32]], axis=0)
+            acc = product(lhs, rhs, acc)
+        return acc
+
+    early = lax.fori_loop(0, NX, early_products, jnp.zeros((64, 96), F32))
+    early = jnp.concatenate([early[0:32] + early[32:64], jnp.zeros((32, 32), F32)], axis=1)
+    early = early + pltpu.roll(early, NZ - 48, 1)
     lane2 = lax.broadcasted_iota(jnp.int32, (K, NZ), 1)
-    th_mine[0] = jnp.where(lane2 < 64, numer, denom)
-    exchange(CORE, 0, th_mine.at[0], th_core)
+    ratio = jnp.where(lane2 < 112, numer, denom)
+    early = jnp.where(lane2 < 48, early[0:16], jnp.where(lane2 < 96, pltpu.roll(early[16:32], 48, 1), ratio))
+    th_mine[0] = early
+    exchange(CORE, 0, th_mine.at[0], th_core)()
     th_mine[1] = th_mine[0] + th_core[0]
-    exchange(PLANE, 1, th_mine.at[1], th_plane)
+    plane_done = exchange(PLANE, 1, th_mine.at[1], th_plane)
+    send("x4")
+
+    receive("x2")
+
+    def power_1(i, j, n, scale):
+        center, beside = around(x_ext, i, j, n)
+        ea[i, pl.ds(j, n)] = scaled(center * (1.0 / 3.0) + beside * (1.0 / 9.0), scale)
+
+    def cross_line(i):
+        for j, n in chunks(H, H + NY):
+            power_1(i, j, n, None)
+
+    def cross(i, carry):
+        power_1(i, H - 1, 1, left)
+        cross_line(i)
+        power_1(i, H + NY, 1, right)
+        return carry
+
+    lax.fori_loop(H, H + NX, cross, 0)
+    pl.when(gx > 0)(lambda: cross_line(H - 1))
+    pl.when(gx < nx - 1)(lambda: cross_line(H + NX))
+
+    def sum_inner(i, j, n, scale):
+        center, beside = around(ea, i, j, n)
+        s_ext[i, pl.ds(j, n)] = x_ext[i, pl.ds(j, n)] + (center * (4.0 / 3.0) + beside * (1.0 / 9.0))
+
+    sweep(0, (NX, NY), H, sum_inner)
+    send("s")
+    plane_done()
     th_mine[2] = tree([th_mine[1]] + [th_plane[i] for i in range(15)])
-    exchange(DEPTH, 16, th_mine.at[2], th_depth)
+    depth_done = exchange(DEPTH, 16, th_mine.at[2], th_depth)
+
+    receive("x4")
+
+    def power_2(i, j, n, scale):
+        center, beside = around(ea, i, j, n)
+        eb[i, pl.ds(j, n)] = scaled(center * (1.0 / 3.0) + beside * (1.0 / 9.0), scale)
+
+    def power_3(i, j, n, scale):
+        center, beside = around(eb, i, j, n)
+        ec[i, pl.ds(j, n)] = scaled(center * (1.0 / 3.0) + beside * (1.0 / 9.0), scale)
+
+    sweep(3, (NX, NY), H, power_1)
+    sweep(2, (NX, NY), H, power_2)
+    sweep(1, (NX, NY), H, power_3)
+    depth_done()
     total = tree([th_mine[2]] + [th_depth[i] for i in range(7)])
-    theta = (total / pltpu.roll(total, 64, 1))[:, 0:1]
-    theta = jnp.broadcast_to(theta, (K, NZ))
-
-    receive("p1")
-
-    def image_p(i, carry):
-        for j, n in chunks(1, 1 + NY):
-            center, beside = around(p_ext, i + 1, j, n)
-            image = 6.0 * center - beside
-            for q in range(n):
-                put(i * NY + j - 1 + q, 64, image[q])
-        return carry
-
-    lax.fori_loop(0, NX, image_p, 0)
-    receive("x4")
-
-    def residual(i, j, n, scale):
-        center, beside = around(x_ext, i, j, n)
-        r_ext[i, pl.ds(j, n)] = scaled((6.0 - theta) * center - beside, scale)
-
-    sweep(3, (NX, NY), H, residual)
-
-    def first_sweep(i, j, n, scale):
-        center, beside = around(r_ext, i, j, n)
-        eb[i, pl.ds(j, n)] = scaled((12.0 * center + beside) * (1.0 / 81.0), scale)
-
-    sweep(2, (NX, NY), H, first_sweep)
-
-    def smoothed(source, i, j, n):
-        center, beside = around(source, i, j, n)
-        return center * (1.0 / 3.0) + (r_ext[i, pl.ds(j, n)] + beside) * (1.0 / 9.0)
-
-    def second_sweep(i, j, n, scale):
-        ec[i, pl.ds(j, n)] = scaled(smoothed(eb, i, j, n), scale)
-
-    def second_row(i):
-        for j, n in chunks(H, H + NY):
-            second_sweep(i, j, n, None)
-
-    sweep_rows = (H, H + NX)
-
-    def second_inner(i, carry):
-        second_sweep(i, H - 1, 1, left)
-        for j, n in chunks(H, H + NY):
-            second_sweep(i, j, n, None)
-        second_sweep(i, H + NY, 1, right)
-        return carry
-
-    lax.fori_loop(sweep_rows[0], sweep_rows[1], second_inner, 0)
-    pl.when(gx > 0)(lambda: second_row(H - 1))
-    pl.when(gx < nx - 1)(lambda: second_row(H + NX))
+    theta = jnp.broadcast_to(total[:, 96:97] / total[:, 112:113], (K, NZ))
+    shifted = 6.0 - theta
 
     def restrict(ci, carry):
         for j, n in chunks(H, H + NY):
             total = None
             for half in range(2):
-                i = 2 * ci + half + H
-                center, beside = around(ec, i, j, n)
-                rest = r_ext[i, pl.ds(j, n)] - 6.0 * center + beside
+                center, beside = around(ec, 2 * ci + half + H, j, n)
+                rest = shifted * center - beside
                 total = rest if total is None else total + rest
             for q in range(0, n, 2):
                 cube = total[q] + total[q + 1]
@@ -363,7 +413,40 @@
 
     lax.fori_loop(0, CX, restrict, 0)
     send("cr")
-    send("e")
+    send("p1")
+
+    def sum_outer(i, j, n):
+        s_ext[i, pl.ds(j, n)] = x_ext[i, pl.ds(j, n)] + ea[i, pl.ds(j, n)] + eb[i, pl.ds(j, n)]
+
+    def sum_sides(i, carry):
+        sum_outer(i, H - 2, 2)
+        sum_outer(i, H + NY, 2)
+        return carry
+
+    lax.fori_loop(H, H + NX, sum_sides, 0)
+    for i in (H - 2, H - 1, H + NX, H + NX + 1):
+        for j, n in chunks(H, H + NY):
+            sum_outer(i, j, n)
+    for i in (H - 1, H + NX):
+        sum_outer(i, H - 1, 1)
+        sum_outer(i, H + NY, 1)
+    receive("s")
+
+    def second_sweep(i, j, n, scale):
+        center, beside = around(s_ext, i, j, n)
+        ec[i, pl.ds(j, n)] = scaled((shifted * center - beside) * (1.0 / 9.0), scale)
+
+    sweep(2, (NX, NY), H, second_sweep)
+
+    def residual(i, j, n, scale):
+        center, beside = around(x_ext, i, j, n)
+        r_ext[i, pl.ds(j, n)] = scaled(shifted * center - beside, scale)
+
+    sweep(2, (NX, NY), H, residual)
+
+    def smoothed(source, i, j, n):
+        center, beside = around(source, i, j, n)
+        return center * (1.0 / 3.0) + (r_ext[i, pl.ds(j, n)] + beside) * (1.0 / 9.0)
 
     receive("cr")
 
@@ -378,13 +461,9 @@
             target[i - shift, pl.ds(j - shift, n)] = scaled(value, scale)
         return body
 
-    sweep(2, (CX, CY), HC, coarse_first)
-    sweep(1, (CX, CY), HC, coarse_next(ca, cb, 0))
-    sweep(0, (CX, CY), HC, coarse_next(cb, cd, HC - HD))
-    send("c")
-    receive("e")
-    receive("c")
-
+    sweep(3, (CX, CY), HC, coarse_first)
+    sweep(2, (CX, CY), HC, coarse_next(ca, cb, 0))
+    sweep(1, (CX, CY), HC, coarse_next(cb, cd, HC - HD))
     def correct(ci, carry):
         for cj in range(CY + 2 * HD):
             packed = cd[ci, cj]
@@ -392,8 +471,8 @@
             high = jnp.where(even[0], pltpu.roll(packed, NZ - 1, 1), packed)
             both = jnp.concatenate([low, high], axis=0)
             for half in range(2):
-                i = 2 * ci + half
-                ea[i, pl.ds(2 * cj, 2)] = ec[i, pl.ds(2 * cj, 2)] + both[None]
+                i, j = 2 * (ci - HD) + half + H, 2 * (cj - HD) + H
+                ea[i, pl.ds(j, 2)] = ec[i, pl.ds(j, 2)] + both[None]
         return carry
 
     lax.fori_loop(0, CX + 2 * HD, correct, 0)
@@ -402,39 +481,90 @@
         eb[i, pl.ds(j, n)] = scaled(smoothed(ea, i, j, n), scale)
 
     def fourth_sweep(i, j, n, scale):
-        ea[i, pl.ds(j, n)] = scaled(smoothed(eb, i, j, n), scale)
-
-    sweep(2, (NX, NY), H, third_sweep)
-    sweep(1, (NX, NY), H, fourth_sweep)
-
-    def image_w(i, carry):
-        for j, n in chunks(H, H + NY):
-            center, beside = around(ea, i + H, j, n)
-            image = 6.0 * center - beside
-            for q in range(n):
-                put(i * NY + j - H + q, 32, center[q])
-                put(i * NY + j - H + q, 80, image[q])
-        return carry
-
-    lax.fori_loop(0, NX, image_w, 0)
-
-    def products(i, acc):
+        value = smoothed(eb, i, j, n)
+        w_ext[i - H + 1, pl.ds(j - H + 1, n)] = value
+        for q in range(n):
+            put((i - H) * NY + j - H + q, W, value[q])
+
+    sweep(1, (NX, NY), H, third_sweep)
+    sweep(0, (NX, NY), H, fourth_sweep)
+    send("w1")
+
+    def half_image(ref, row):
+        def double(i, carry):
+            ref[i, 0] = ref[i, 0] * 2.0
+            return carry
+
+        lax.fori_loop(1, 1 + NX, double, 0)
+        for j, n in chunks(1, 1 + NY):
+            ref[0, pl.ds(j, n)] = ref[0, pl.ds(j, n)] * 2.0
+
+        def image_row(i, carry):
+            for j, n in chunks(1, 1 + NY):
+                center, beside = around(ref, i + 1, j, n)
+                image = 6.0 * center - beside
+                for q in range(n):
+                    put(i * NY + j - 1 + q, row, image[q])
+            return carry
+
+        lax.fori_loop(0, NX, image_row, 0)
+
+    receive("p1")
+    half_image(p_ext, IP)
+
+    def late_products(i, acc):
         for j in range(0, NY, 2):
             cell = i * NY + j
-            rhs = jnp.concatenate([split[cell], split[cell + 1]], axis=1)
-            lhs = jnp.concatenate([rhs[0:48], rhs[128:176]], axis=0)
-            acc = acc + lax.dot_general(lhs, rhs, (((1,), (1,)), ((), ())), preferred_element_type=F32)
+            high, low = pair(cell, X, 80), pair(cell, X + 128, 80)
+            rhs = jnp.concatenate([high[48:80], low[48:80]], axis=0)
+            acc = product(jnp.concatenate([high, low], axis=0), rhs, acc)
         return acc
 
-    acc = lax.fori_loop(0, NX, products, jnp.zeros((96, 256), F32))
-    part = (acc[0:48, 0:128] + acc[0:48, 128:256]) + (acc[48:96, 0:128] + acc[48:96, 128:256])
-    ar_mine[0] = part[0:24]
-    ar_mine[1] = part[24:48]
-    exchange(CORE, 23, ar_mine.at[1 - core], ar_core)
+    late = lax.fori_loop(0, NX, late_products, jnp.zeros((160, 64), F32))
+    receive("w1")
+    half_image(w_ext, IW)
+
+    def last_products(i, acc):
+        for j in range(0, NY, 2):
+            cell = i * NY + j
+            rhs = jnp.concatenate([pair(cell, IW, 16), pair(cell, IW + 128, 16)], axis=0)
+            lhs = [pair(cell, row, 16) for row in (PD, W, PD + 128, W + 128)]
+            acc = product(jnp.concatenate(lhs, axis=0), rhs, acc)
+        return acc
+
+    last = lax.fori_loop(0, NX, last_products, jnp.zeros((64, 32), F32))
+
+    def folded(value, half, width):
+        value = value[0:half] + value[half : 2 * half]
+        value = jnp.concatenate([value, jnp.zeros((half, NZ - 2 * width), F32)], axis=1)
+        return value + pltpu.roll(value, NZ - width, 1)
+
+    late = folded(late, 80, 32)
+    last = folded(last, 32, 16)
+
+    def moved(value, start, end):
+        return pltpu.roll(value, (end - start) % NZ, 1) if start != end else value
+
+    mixed = 0.5 * (moved(late[48:64], 16, 48) + moved(last[0:16], 0, 48))
+    blocks = [
+        moved(late[0:16], 16, 0),
+        late[32:48],
+        moved(late[16:32], 16, 32),
+        mixed,
+        moved(late[64:80], 16, 64),
+        moved(last[16:32], 0, 80),
+        moved(late[16:32], 0, 96),
+    ]
+    part = jnp.zeros((K, NZ), F32)
+    for index, block in enumerate(blocks):
+        part = jnp.where(lane2 // K == index, block, part)
+    ar_mine[0] = part[0:8]
+    ar_mine[1] = part[8:16]
+    exchange(CORE, 23, ar_mine.at[1 - core], ar_core)()
     ar_mine[2] = ar_mine[core] + ar_core[0]
-    exchange(PLANE, 24, ar_mine.at[2], ar_plane)
+    exchange(PLANE, 24, ar_mine.at[2], ar_plane)()
     ar_mine[3] = tree([ar_mine[2]] + [ar_plane[i] for i in range(15)])
-    exchange(DEPTH, 39, ar_mine.at[3], ar_depth)
+    exchange(DEPTH, 39, ar_mine.at[3], ar_depth)()
     ar_full[core] = tree([ar_mine[3]] + [ar_depth[i] for i in range(7)])
     swap = pltpu.make_async_remote_copy(
         src_ref=ar_full.at[core],
@@ -475,9 +605,27 @@
     def dot_t(a, b):
         return lax.dot_general(a, b, (((1,), (1,)), ((), ())), precision=HP, preferred_element_type=F32)
 
-    proj = pltpu.roll(both, NZ - 48, 1)[:, 0:48]
+    rows = lax.broadcasted_iota(jnp.int32, (48, 48), 0)
+    cols = lax.broadcasted_iota(jnp.int32, (48, 48), 1)
+
+    def upper(first, second, third):
+        return jnp.concatenate([first, second, third], axis=0)[:, 0:48]
+
+    x_rows, p_rows = total, moved(total, 48, 0)
+    gram = upper(
+        jnp.where(lane2 < 32, x_rows, moved(both, 0, 32)), jnp.where(lane2 < 32, p_rows, both), moved(both, 64, 32)
+    )
+    gram = jnp.where(jnp.logical_and(rows >= 32, cols < 32), gram.T, gram)
+    proj = upper(
+        jnp.where(lane2 < 32, moved(x_rows, 32, 0), moved(both, 16, 32)),
+        jnp.where(lane2 < 16, moved(p_rows, 32, 0), jnp.where(lane2 < 32, moved(both, 96, 16), moved(both, 48, 32))),
+        moved(both, 80, 32),
+    )
+    below = jnp.logical_and(rows >= 32, cols < 32)
+    beside_x = jnp.logical_and(rows < 16, jnp.logical_and(cols >= 16, cols < 32))
+    proj = jnp.where(jnp.logical_or(below, beside_x), proj.T, proj)
     proj = 0.5 * (proj + proj.T)
-    lower_inv = inverse_factor(both, 48)
+    lower_inv = inverse_factor(jnp.concatenate([gram, jnp.zeros((48, NZ - 48), F32)], axis=1), 48)
     ritz = dot_t(dot(lower_inv, proj), lower_inv)
     ritz = 0.5 * (ritz + ritz.T)
     rows = lax.broadcasted_iota(jnp.int32, (K, 48), 0)
@@ -490,7 +638,8 @@
     coef_t = dot(dot(small_inv, filtered_t), lower_inv) * (ncells**0.5)
 
     coef_t = jnp.concatenate([coef_t, jnp.where(cols < K, 0.0, coef_t)], axis=0)
-    coef_t = jnp.concatenate([coef_t, jnp.zeros((2 * K, NZ - 48), F32)], axis=1)
+    gap = jnp.zeros((2 * K, 32), F32)
+    coef_t = jnp.concatenate([coef_t[:, 0:32], gap, coef_t[:, 32:48], gap, gap[:, 0:16]], axis=1)
     high = coef_t.astype(BF16)
     low = (coef_t - high.astype(F32)).astype(BF16)
     weights = jnp.concatenate([high, low], axis=0)
@@ -529,6 +678,8 @@
         vmem(flat, F32),
         vmem(fine, F32),
         vmem((NX + 2, NY + 2, K, NZ), F32),
+        vmem((NX + 2, NY + 2, K, NZ), F32),
+        vmem(fine, F32),
         vmem(fine, F32),
         vmem(fine, F32),
         vmem(fine, F32),
@@ -544,11 +695,11 @@
         vmem((1, K, NZ), F32),
         vmem((15, K, NZ), F32),
         vmem((7, K, NZ), F32),
-        vmem((4, 24, NZ), F32),
-        vmem((1, 24, NZ), F32),
-        vmem((15, 24, NZ), F32),
-        vmem((7, 24, NZ), F32),
-        vmem((2, 24, NZ), F32),
+        vmem((4, 8, NZ), F32),
+        vmem((1, 8, NZ), F32),
+        vmem((15, 8, NZ), F32),
+        vmem((7, 8, NZ), F32),
+        vmem((2, 8, NZ), F32),
         pltpu.SemaphoreType.DMA((COUNT,)),
         pltpu.SemaphoreType.DMA((COUNT,)),
         pltpu.SemaphoreType.DMA((47,)),

time: 119 us -> 105 us (0.88)
  Pallas kernels: 115 us -> 100 us
    pallas_call x1, Pallas kernels: 115 us -> 100 us  [body(): pl.pallas_call(kernel, out_shape=(jax.ShapeDtypeStruct(flat, F32), jax.Sh...]
where the time goes in v1:
time: 105 us; the launch traced here: 104 us
  Pallas kernels  100 us (95%)
  local copies, waits for them, and re-layouts  3.36 us (3%)
    pallas_call x1, Pallas kernels, body(): pl.pallas_call(kernel, out_shape=(jax.ShapeDtypeStruct(flat, F32), jax.Sh...  100 us
    unnamed x4, local copies, waits for them, and re-layouts  3.36 us

profile of v1, /device:TPU:1, one launch (start us, length us, event | category | flops | bytes accessed | tf_op | source)
XLA Modules:
  0.0 104.4 jit_solution(8276607657561055488)
XLA Ops:
  0.6 100.4 %shard_map.41 = (f32[2048,128]{1,0:T(8,128)}, f32[2048,128]{1,0:T(8,128)}) custom-call(f32[2048,128]{1,0:T(8,128)} %bitcast.4, f32[2048,128]{1,0:T(8,128)} %bitcast.5), custom_call_target="tpu_custom_call" | custom-call | tf_op jit(solution)/shard_map/pallas_call | solution.py:709
  101.0 0.0 copy-start
  101.0 2.4 %copy.6 = f32[16,8,16,128]{3,2,1,0:T(8,128)} copy(f32[16,8,16,128]{3,2,1,0:T(8,128)} %bitcast.7) | data formatting | bytes 2097152
  103.4 0.0 copy-done
  103.4 1.0 copy.7
Async XLA Ops:
  101.0 2.4 %copy-start = (f32[2048,128]{1,0:T(8,128)S(1)}, f32[2048,128]{1,0:T(8,128)}, u32[]{:S(2)}) copy-start(f32[2048,128]{1,0:T(8,128)} %get-tuple-element.5) | copy-start | bytes 3145732

commit v2 on v1

--- a/solution.py
+++ b/solution.py
@@ -448,6 +448,36 @@
         center, beside = around(source, i, j, n)
         return center * (1.0 / 3.0) + (r_ext[i, pl.ds(j, n)] + beside) * (1.0 / 9.0)
 
+    def inverse_factor(matrix, size):
+        rows = lax.broadcasted_iota(jnp.int32, (size, NZ), 0)
+        lanes = lax.broadcasted_iota(jnp.int32, (size, NZ), 1)
+        start = jnp.where(lanes < size, matrix, jnp.where(lanes == rows + 64, 1.0, 0.0))
+        tiles = [start[8 * t : 8 * t + 8] for t in range(size // 8)]
+        sub = lax.broadcasted_iota(jnp.int32, (8, NZ), 0)
+        for k in range(size):
+            t0, s0 = k // 8, k % 8
+            pivot = tiles[t0][s0 : s0 + 1]
+            pivot = pivot / pivot[:, k : k + 1]
+            for t in range(t0, size // 8):
+                column = jnp.broadcast_to(tiles[t][:, k : k + 1], (8, NZ))
+                if t == t0:
+                    column = jnp.where(sub > s0, column, 0.0)
+                tiles[t] = tiles[t] - column * pivot
+        done = jnp.concatenate(tiles, axis=0)
+        diagonal = jnp.sum(jnp.where(lanes == rows, done, 0.0), axis=1, keepdims=True)
+        return pltpu.roll(done / jnp.sqrt(diagonal), 64, 1)[:, 0:size]
+
+    def dot(a, b):
+        return jnp.dot(a, b, precision=HP, preferred_element_type=F32)
+
+    def dot_t(a, b):
+        return lax.dot_general(a, b, (((1,), (1,)), ((), ())), precision=HP, preferred_element_type=F32)
+
+    def moved(value, start, end):
+        return pltpu.roll(value, (end - start) % NZ, 1) if start != end else value
+
+    first_inv = inverse_factor(jnp.concatenate([total, moved(total, 48, 0)], axis=0), 32)
+
     receive("cr")
 
     def coarse_first(i, j, n, scale):
@@ -541,9 +571,6 @@
 
     late = folded(late, 80, 32)
     last = folded(last, 32, 16)
-
-    def moved(value, start, end):
-        return pltpu.roll(value, (end - start) % NZ, 1) if start != end else value
 
     mixed = 0.5 * (moved(late[48:64], 16, 48) + moved(last[0:16], 0, 48))
     blocks = [
@@ -580,31 +607,6 @@
 
     both = jnp.concatenate([ar_full[0], ar_full[1]], axis=0)
 
-    def inverse_factor(matrix, size):
-        rows = lax.broadcasted_iota(jnp.int32, (size, NZ), 0)
-        lanes = lax.broadcasted_iota(jnp.int32, (size, NZ), 1)
-        start = jnp.where(lanes < size, matrix, jnp.where(lanes == rows + 64, 1.0, 0.0))
-        tiles = [start[8 * t : 8 * t + 8] for t in range(size // 8)]
-        sub = lax.broadcasted_iota(jnp.int32, (8, NZ), 0)
-        for k in range(size):
-            t0, s0 = k // 8, k % 8
-            pivot = tiles[t0][s0 : s0 + 1]
-            pivot = pivot / pivot[:, k : k + 1]
-            for t in range(t0, size // 8):
-                column = jnp.broadcast_to(tiles[t][:, k : k + 1], (8, NZ))
-                if t == t0:
-                    column = jnp.where(sub > s0, column, 0.0)
-                tiles[t] = tiles[t] - column * pivot
-        done = jnp.concatenate(tiles, axis=0)
-        diagonal = jnp.sum(jnp.where(lanes == rows, done, 0.0), axis=1, keepdims=True)
-        return pltpu.roll(done / jnp.sqrt(diagonal), 64, 1)[:, 0:size]
-
-    def dot(a, b):
-        return jnp.dot(a, b, precision=HP, preferred_element_type=F32)
-
-    def dot_t(a, b):
-        return lax.dot_general(a, b, (((1,), (1,)), ((), ())), precision=HP, preferred_element_type=F32)
-
     rows = lax.broadcasted_iota(jnp.int32, (48, 48), 0)
     cols = lax.broadcasted_iota(jnp.int32, (48, 48), 1)
 
@@ -612,10 +614,6 @@
         return jnp.concatenate([first, second, third], axis=0)[:, 0:48]
 
     x_rows, p_rows = total, moved(total, 48, 0)
-    gram = upper(
-        jnp.where(lane2 < 32, x_rows, moved(both, 0, 32)), jnp.where(lane2 < 32, p_rows, both), moved(both, 64, 32)
-    )
-    gram = jnp.where(jnp.logical_and(rows >= 32, cols < 32), gram.T, gram)
     proj = upper(
         jnp.where(lane2 < 32, moved(x_rows, 32, 0), moved(both, 16, 32)),
         jnp.where(lane2 < 16, moved(p_rows, 32, 0), jnp.where(lane2 < 32, moved(both, 96, 16), moved(both, 48, 32))),
@@ -625,7 +623,18 @@
     beside_x = jnp.logical_and(rows < 16, jnp.logical_and(cols >= 16, cols < 32))
     proj = jnp.where(jnp.logical_or(below, beside_x), proj.T, proj)
     proj = 0.5 * (proj + proj.T)
-    lower_inv = inverse_factor(jnp.concatenate([gram, jnp.zeros((48, NZ - 48), F32)], axis=1), 48)
+    with_w = jnp.concatenate([both, moved(both, 32, 0)], axis=0)[:, 0:K]
+    below_t = dot(first_inv, with_w).T
+    schur = moved(both, 64, 0)[:, 0:K] - dot_t(below_t, below_t)
+    last_inv = inverse_factor(jnp.concatenate([schur, jnp.zeros((K, NZ - K), F32)], axis=1), K)
+    corner = dot(last_inv, dot(below_t, first_inv))
+    lower_inv = jnp.concatenate(
+        [
+            jnp.concatenate([first_inv, jnp.zeros((32, K), F32)], axis=1),
+            jnp.concatenate([-corner, last_inv], axis=1),
+        ],
+        axis=0,
+    )
     ritz = dot_t(dot(lower_inv, proj), lower_inv)
     ritz = 0.5 * (ritz + ritz.T)
     rows = lax.broadcasted_iota(jnp.int32, (K, 48), 0)

time: 105 us -> 102 us (0.971)
  Pallas kernels: 100 us -> 98.2 us
    pallas_call x1, Pallas kernels: 100 us -> 98.2 us  [body(): pl.pallas_call(kernel, out_shape=(jax.ShapeDtypeStruct(flat, F32), jax.Sh...]
where the time goes in v2:
time: 102 us
  Pallas kernels  98.2 us (96%)
  local copies, waits for them, and re-layouts  3.36 us (3%)
    pallas_call x1, Pallas kernels, body(): pl.pallas_call(kernel, out_shape=(jax.ShapeDtypeStruct(flat, F32), jax.Sh...  98.2 us
    unnamed x4, local copies, waits for them, and re-layouts  3.36 us

profile of v2, /device:TPU:1, one launch (start us, length us, event | category | flops | bytes accessed | tf_op | source)
XLA Modules:
  0.0 102.2 jit_solution(17556711411297344384)
XLA Ops:
  0.6 98.2 %shard_map.41 = (f32[2048,128]{1,0:T(8,128)}, f32[2048,128]{1,0:T(8,128)}) custom-call(f32[2048,128]{1,0:T(8,128)} %bitcast.4, f32[2048,128]{1,0:T(8,128)} %bitcast.5), custom_call_target="tpu_custom_call" | custom-call | tf_op jit(solution)/shard_map/pallas_call | solution.py:718
  98.8 0.0 copy-start
  98.8 2.4 %copy.6 = f32[16,8,16,128]{3,2,1,0:T(8,128)} copy(f32[16,8,16,128]{3,2,1,0:T(8,128)} %bitcast.7) | data formatting | bytes 2097152
  101.2 0.0 copy-done
  101.2 1.0 copy.7
Async XLA Ops:
  98.8 2.4 %copy-start = (f32[2048,128]{1,0:T(8,128)S(1)}, f32[2048,128]{1,0:T(8,128)}, u32[]{:S(2)}) copy-start(f32[2048,128]{1,0:T(8,128)} %get-tuple-element.5) | copy-start | bytes 3145732

commit v3 on v2

--- a/solution.py
+++ b/solution.py
@@ -50,7 +50,8 @@
     groups = {}
     groups["x1"] = [("x", d, (1, 1), (1, 1)) for d in range(4)]
     groups["x2"] = [("x", d, (2, 2), (2, 2)) for d in range(4)] + [("x", d, (1, 1), (1, 1)) for d in range(4, 8)]
-    deep = [("x", d, (3, 4), (3, 4)) for d in range(4)]
+    groups["x3"] = [("x", d, (3, 3), (3, 3)) for d in range(4)]
+    deep = [("x", d, (4, 4), (4, 4)) for d in range(4)]
     for d in range(4, 8):
         deep += [("x", d, (1, 1), (2, 3)), ("x", d, (2, 2), (1, 2)), ("x", d, (3, 3), (1, 1))]
     groups["x4"] = deep
@@ -237,6 +238,7 @@
     pl.semaphore_wait(barrier, expected + len(partners))
     send("x1")
     send("x2")
+    send("x3")
     load_p.wait()
     clear(r_ext, H)
     clear(ea, H)
@@ -378,6 +380,7 @@
     th_mine[2] = tree([th_mine[1]] + [th_plane[i] for i in range(15)])
     depth_done = exchange(DEPTH, 16, th_mine.at[2], th_depth)
 
+    receive("x3")
     receive("x4")
 
     def power_2(i, j, n, scale):

time: 102 us -> 99.6 us (0.976)
  Pallas kernels: 98.2 us -> 95.5 us
    pallas_call x1, Pallas kernels: 98.2 us -> 95.5 us  [body(): pl.pallas_call(kernel, out_shape=(jax.ShapeDtypeStruct(flat, F32), jax.Sh...]
where the time goes in v3:
time: 99.6 us; the launch traced here: 99.5 us
  Pallas kernels  95.5 us (96%)
  local copies, waits for them, and re-layouts  3.36 us (3%)
    pallas_call x1, Pallas kernels, body(): pl.pallas_call(kernel, out_shape=(jax.ShapeDtypeStruct(flat, F32), jax.Sh...  95.5 us
    unnamed x4, local copies, waits for them, and re-layouts  3.36 us

profile of v3, /device:TPU:1, one launch (start us, length us, event | category | flops | bytes accessed | tf_op | source)
XLA Modules:
  0.0 99.5 jit_solution(5315517980279634967)
XLA Ops:
  0.6 95.5 %shard_map.41 = (f32[2048,128]{1,0:T(8,128)}, f32[2048,128]{1,0:T(8,128)}) custom-call(f32[2048,128]{1,0:T(8,128)} %bitcast.4, f32[2048,128]{1,0:T(8,128)} %bitcast.5), custom_call_target="tpu_custom_call" | custom-call | tf_op jit(solution)/shard_map/pallas_call | solution.py:721
  96.1 0.0 copy-start
  96.1 2.4 %copy.6 = f32[16,8,16,128]{3,2,1,0:T(8,128)} copy(f32[16,8,16,128]{3,2,1,0:T(8,128)} %bitcast.7) | data formatting | bytes 2097152
  98.5 0.0 copy-done
  98.5 1.0 copy.7
Async XLA Ops:
  96.1 2.4 %copy-start = (f32[2048,128]{1,0:T(8,128)S(1)}, f32[2048,128]{1,0:T(8,128)}, u32[]{:S(2)}) copy-start(f32[2048,128]{1,0:T(8,128)} %get-tuple-element.5) | copy-start | bytes 3145732

commit v4 on v3

--- a/solution.py
+++ b/solution.py
@@ -416,7 +416,6 @@
 
     lax.fori_loop(0, CX, restrict, 0)
     send("cr")
-    send("p1")
 
     def sum_outer(i, j, n):
         s_ext[i, pl.ds(j, n)] = x_ext[i, pl.ds(j, n)] + ea[i, pl.ds(j, n)] + eb[i, pl.ds(j, n)]
@@ -482,6 +481,7 @@
     first_inv = inverse_factor(jnp.concatenate([total, moved(total, 48, 0)], axis=0), 32)
 
     receive("cr")
+    send("p1")
 
     def coarse_first(i, j, n, scale):
         center, beside = around(crp, i, j, n, 2)

time: 99.6 us -> 98.1 us (0.985)
  Pallas kernels: 95.5 us -> 94 us
    pallas_call x1, Pallas kernels: 95.5 us -> 94 us  [body(): pl.pallas_call(kernel, out_shape=(jax.ShapeDtypeStruct(flat, F32), jax.Sh...]
where the time goes in v4:
time: 98.1 us; the launch traced here: 98 us
  Pallas kernels  94 us (96%)
  local copies, waits for them, and re-layouts  3.36 us (3%)
    pallas_call x1, Pallas kernels, body(): pl.pallas_call(kernel, out_shape=(jax.ShapeDtypeStruct(flat, F32), jax.Sh...  94 us
    unnamed x4, local copies, waits for them, and re-layouts  3.36 us

profile of v4, /device:TPU:1, one launch (start us, length us, event | category | flops | bytes accessed | tf_op | source)
XLA Modules:
  0.0 98.0 jit_solution(8159218132519632022)
XLA Ops:
  0.6 94.0 %shard_map.41 = (f32[2048,128]{1,0:T(8,128)}, f32[2048,128]{1,0:T(8,128)}) custom-call(f32[2048,128]{1,0:T(8,128)} %bitcast.4, f32[2048,128]{1,0:T(8,128)} %bitcast.5), custom_call_target="tpu_custom_call" | custom-call | tf_op jit(solution)/shard_map/pallas_call | solution.py:721
  94.6 0.0 copy-start
  94.6 2.4 %copy.6 = f32[16,8,16,128]{3,2,1,0:T(8,128)} copy(f32[16,8,16,128]{3,2,1,0:T(8,128)} %bitcast.7) | data formatting | bytes 2097152
  97.0 0.0 copy-done
  97.0 1.0 copy.7
Async XLA Ops:
  94.6 2.4 %copy-start = (f32[2048,128]{1,0:T(8,128)S(1)}, f32[2048,128]{1,0:T(8,128)}, u32[]{:S(2)}) copy-start(f32[2048,128]{1,0:T(8,128)} %get-tuple-element.5) | copy-start | bytes 3145732
